TPU v7x, 256 devices: a whole 4x4x8 slice. The times are simulated.
256 devices in a mesh: sweep: 8 (over y, core), leaf: 32 (over z, x).
Axes of the slice: x: 4, y: 4, z: 8, core: 2. Of those that a mesh axis runs over, the one named last changes fastest.
Arguments:
- rhs: bfloat16 [8, 256, 32, 512], P('sweep', 'leaf'), may hold values from -6 to 6
- incoming: bfloat16 [256, 32, 512], P('leaf'), may hold values from -6 to 6
- front_inv: bfloat16 [8, 256, 2, 256, 256], P('sweep', 'leaf'), may hold values from -0.21875 to 0.21875
- coupling: bfloat16 [8, 256, 2, 256, 256], P('sweep', 'leaf'), may hold values from -0.25 to 0.25
- update: bfloat16 [8, 256, 4, 2, 256, 256], P('sweep', 'leaf'), may hold values from -0.09375 to 0.09375
- dest_owner: int32 [256, 4], P('leaf'), may hold values from 0 to 31, all different within a row; in each aligned block of 8 rows (0 to 7, 8 to 15, ...) at most 2 rows name the same one
- dest_front: int32 [256, 4], P('leaf'), may hold values from 0 to 7
Outputs:
- solution: bfloat16 [8, 256, 32, 512], P('sweep', 'leaf')
Inputs may be any that keep to these rules, and one draw needn't show every extreme that they name: `dest_owner`: among the rows of one index of leaf no owner is named more than 2 times, and that bound is reached; a front names 4 different owners.
All inputs are finite; a program needn't handle non-finite values.
Results may differ from a plain program's by a relative error of at most 0.03.
Values may be sent and summed in bfloat16 or wider, within the bound.
A program may use at most 128 MiB of HBM per device.

v0:
```python
import jax
import jax.numpy as jnp
from jax import lax
from jax.sharding import PartitionSpec as P


def shifted(value, axis, by):
    size = lax.axis_size(axis)
    pairs = [(i, i + by) for i in range(size) if 0 <= i + by < size]
    return lax.ppermute(value, axis, pairs)


def complex_apply(vectors, matrix):
    width = matrix.shape[-1]
    real_in = vectors[..., :width]
    imag_in = vectors[..., width:]
    real_mat = matrix[..., 0, :, :]
    imag_mat = matrix[..., 1, :, :]
    real_out = jnp.matmul(real_in, real_mat, preferred_element_type=jnp.float32) - jnp.matmul(
        imag_in, imag_mat, preferred_element_type=jnp.float32
    )
    imag_out = jnp.matmul(real_in, imag_mat, preferred_element_type=jnp.float32) + jnp.matmul(
        imag_in, real_mat, preferred_element_type=jnp.float32
    )
    return jnp.concatenate([real_out, imag_out], axis=-1)


def body(rhs, incoming, front_inv, coupling, update, dest_owner, dest_front):
    leaf_count = lax.axis_size("leaf")
    sweep_count = lax.axis_size("sweep")
    sweep_me = lax.axis_index("sweep")
    fronts_here = rhs.shape[1]
    total_rows = rhs.shape[2]
    doubled = rhs.shape[3]
    blocks_each = dest_owner.shape[1]
    pairs = fronts_here * blocks_each
    bound = min(fronts_here - 1, max(2, 2 * fronts_here * blocks_each // leaf_count))
    slots = leaf_count * bound
    owners = dest_owner.reshape(pairs)
    local_targets = dest_front.reshape(pairs)
    owner_table = (owners[:, None] == jnp.arange(leaf_count, dtype=jnp.int32)[None, :]).astype(
        jnp.int32
    )
    earlier = jnp.cumsum(owner_table, axis=0) - owner_table
    ranking = jnp.sum(earlier * owner_table, axis=1)
    slot_of = owners * bound + ranking
    placing = (slot_of[None, :] == jnp.arange(slots, dtype=jnp.int32)[:, None]).astype(jnp.int32)
    placing_half = placing.astype(jnp.bfloat16)

    def receive_table(targets):
        return (targets[None, :] == jnp.arange(fronts_here, dtype=jnp.int32)[:, None]).astype(
            jnp.bfloat16
        )

    occupied = jnp.sum(placing, axis=1)
    chosen_local = jnp.sum(placing * local_targets[None, :], axis=1)
    sent_targets = jnp.where(occupied > 0, chosen_local, fronts_here).reshape(leaf_count, bound)

    def solve(previous, rhs_rows):
        rows = rhs_rows.shape[1]
        field = rhs_rows.astype(jnp.float32) - complex_apply(previous, coupling[0])
        field_half = field.astype(jnp.bfloat16)
        first = complex_apply(field_half, front_inv[0]).astype(jnp.bfloat16)
        contribution = complex_apply(first[:, None], update[0]).astype(jnp.bfloat16)
        contribution = contribution.reshape(pairs, rows, doubled)
        outgoing = jnp.einsum(
            "sp,prc->src", placing_half, contribution, preferred_element_type=jnp.float32
        )
        outgoing = outgoing.astype(jnp.bfloat16).reshape(leaf_count, bound, rows, doubled)
        arrived, arrived_targets = (
            lax.all_to_all(outgoing, "leaf", split_axis=0, concat_axis=0, tiled=True),
            lax.all_to_all(sent_targets, "leaf", split_axis=0, concat_axis=0, tiled=True),
        )
        table = receive_table(arrived_targets.reshape(slots))
        summed = jnp.einsum(
            "js,src->jrc",
            table,
            arrived.reshape(slots, rows, doubled),
            preferred_element_type=jnp.float32,
        )
        remainder = (field - summed).astype(jnp.bfloat16)
        return complex_apply(remainder, front_inv[0]).astype(jnp.bfloat16)

    group_count = total_rows // total_rows
    steps = sweep_count + group_count - 1

    def advance(step, carry):
        previous, result = carry
        group = step - sweep_me
        valid = (group >= 0) & (group < group_count)
        rhs_rows = rhs[0]
        used = jnp.where(sweep_me == 0, incoming, previous)
        solved = solve(used, rhs_rows)
        result = jnp.where(valid, solved, result)
        previous = shifted(solved, "sweep", 1)
        return (previous, result)

    initial = (jnp.zeros((fronts_here, total_rows, doubled), jnp.bfloat16), jnp.zeros_like(rhs[0]))
    final = lax.fori_loop(0, steps, advance, initial)
    return final[1][None]


def solution(mesh):
    return jax.shard_map(
        body,
        mesh=mesh,
        in_specs=(
            P("sweep", "leaf", None, None),
            P("leaf", None, None),
            P("sweep", "leaf", None, None, None),
            P("sweep", "leaf", None, None, None),
            P("sweep", "leaf", None, None, None, None),
            P("leaf", None),
            P("leaf", None),
        ),
        out_specs=P("sweep", "leaf", None, None),
        check_vma=False,
    )
```

profile of v0, /device:TPU:10, one launch (start us, length us, event | category | flops | bytes accessed | tf_op | source)
XLA Modules:
  0.0 791.0 jit_solution(5895066867643698199)
XLA Ops:
  2.8 11.6 %all-to-all-start.1 = ((s32[32,1,2]{2,1,0:T(1,128)}), s32[32,1,2]{2,1,0:T(1,128)S(1)}, u32[]{:S(2)}, u32[]{:S(2)}) async-start(s32[32,1,2]{2,1,0:T(1,128)} %bitcast), calls=%async_computation.1 | async-start | bytes 32768 | tf_op jit(solution)/shard_map/while/body/eval_jaxpr/all_to_all | solution.py:72
  14.5 7.7 copy.47
  25.5 764.8 %while.19 = (s32[]{:T(128)}, bf16[8,32,512]{2,1,0:T(8,128)(2,1)S(1)}, bf16[8,32,512]{2,1,0:T(8,128)(2,1)S(1)}, bf16[1,8,32,512]{3,2,1,0:T(8,128)(2,1)S(1)}, pred...) while((s32[]{:T(128)}, ...), condition=%wide.wide.region_5.6_spmd.clone, body=%wide.wide.region_4.5_spmd.clone.sunk | while | flops 1030363648 | bytes 119276216 | solution.py:99
  46.5 9.8 %all-to-all-start = ((bf16[32,2,32,512]{3,1,2,0:T(2,128)(2,1)}), bf16[32,2,32,512]{3,1,2,0:T(2,128)(2,1)}, u32[]{:S(2)}, u32[]{:S(2)}) async-start(bf16[32,2,32,512]{3,1,2,0:T(2,128)(2,1)} %copy.66), calls=%async_computation | async-start | bytes 4194304 | tf_op jit(solution)/shard_map/while/body/eval_jaxpr/all_to_all | solution.py:71
  56.3 48.8 %all-to-all-done = bf16[32,2,32,512]{3,1,2,0:T(2,128)(2,1)} async-done(((bf16[32,2,32,512]{3,1,2,0:T(2,128)(2,1)}), bf16[32,2,32,512]{3,1,2,0:T(2,128)(2,1)}, u32[]{:S(2)}, u32[]{:S(2)}) %all-to-all-start) | async-done | bytes 2097184 | tf_op jit(solution)/shard_map/while/body/eval_jaxpr/all_to_all | solution.py:71
  105.2 5.1 copy.67
  120.0 5.8 collective-permute-done
  146.7 6.8 all-to-all-start
  153.5 48.8 %all-to-all-done = bf16[32,2,32,512]{3,1,2,0:T(2,128)(2,1)} async-done(((bf16[32,2,32,512]{3,1,2,0:T(2,128)(2,1)}), bf16[32,2,32,512]{3,1,2,0:T(2,128)(2,1)}, u32[]{:S(2)}, u32[]{:S(2)}) %all-to-all-start) | async-done | bytes 2097184 | tf_op jit(solution)/shard_map/while/body/eval_jaxpr/all_to_all | solution.py:71
  202.3 5.1 copy.67
  217.1 5.8 collective-permute-done
  243.8 6.8 all-to-all-start
  250.6 48.6 %all-to-all-done = bf16[32,2,32,512]{3,1,2,0:T(2,128)(2,1)} async-done(((bf16[32,2,32,512]{3,1,2,0:T(2,128)(2,1)}), bf16[32,2,32,512]{3,1,2,0:T(2,128)(2,1)}, u32[]{:S(2)}, u32[]{:S(2)}) %all-to-all-start) | async-done | bytes 2097184 | tf_op jit(solution)/shard_map/while/body/eval_jaxpr/all_to_all | solution.py:71
  299.3 5.1 copy.67
  314.0 5.8 collective-permute-done
  340.8 6.6 all-to-all-start
  347.4 45.9 %all-to-all-done = bf16[32,2,32,512]{3,1,2,0:T(2,128)(2,1)} async-done(((bf16[32,2,32,512]{3,1,2,0:T(2,128)(2,1)}), bf16[32,2,32,512]{3,1,2,0:T(2,128)(2,1)}, u32[]{:S(2)}, u32[]{:S(2)}) %all-to-all-start) | async-done | bytes 2097184 | tf_op jit(solution)/shard_map/while/body/eval_jaxpr/all_to_all | solution.py:71
  408.1 5.8 collective-permute-done
  434.9 5.7 all-to-all-start
  440.6 47.0 %all-to-all-done = bf16[32,2,32,512]{3,1,2,0:T(2,128)(2,1)} async-done(((bf16[32,2,32,512]{3,1,2,0:T(2,128)(2,1)}), bf16[32,2,32,512]{3,1,2,0:T(2,128)(2,1)}, u32[]{:S(2)}, u32[]{:S(2)}) %all-to-all-start) | async-done | bytes 2097184 | tf_op jit(solution)/shard_map/while/body/eval_jaxpr/all_to_all | solution.py:71
  502.4 5.8 collective-permute-done
  529.1 5.6 all-to-all-start
  534.7 45.8 %all-to-all-done = bf16[32,2,32,512]{3,1,2,0:T(2,128)(2,1)} async-done(((bf16[32,2,32,512]{3,1,2,0:T(2,128)(2,1)}), bf16[32,2,32,512]{3,1,2,0:T(2,128)(2,1)}, u32[]{:S(2)}, u32[]{:S(2)}) %all-to-all-start) | async-done | bytes 2097184 | tf_op jit(solution)/shard_map/while/body/eval_jaxpr/all_to_all | solution.py:71
  580.6 5.1 copy.67
  595.3 5.8 collective-permute-done
  622.1 6.3 all-to-all-start
  628.4 45.8 %all-to-all-done = bf16[32,2,32,512]{3,1,2,0:T(2,128)(2,1)} async-done(((bf16[32,2,32,512]{3,1,2,0:T(2,128)(2,1)}), bf16[32,2,32,512]{3,1,2,0:T(2,128)(2,1)}, u32[]{:S(2)}, u32[]{:S(2)}) %all-to-all-start) | async-done | bytes 2097184 | tf_op jit(solution)/shard_map/while/body/eval_jaxpr/all_to_all | solution.py:71
  689.0 5.8 collective-permute-done
  715.7 6.3 all-to-all-start
  722.0 45.8 %all-to-all-done = bf16[32,2,32,512]{3,1,2,0:T(2,128)(2,1)} async-done(((bf16[32,2,32,512]{3,1,2,0:T(2,128)(2,1)}), bf16[32,2,32,512]{3,1,2,0:T(2,128)(2,1)}, u32[]{:S(2)}, u32[]{:S(2)}) %all-to-all-start) | async-done | bytes 2097184 | tf_op jit(solution)/shard_map/while/body/eval_jaxpr/all_to_all | solution.py:71
  767.9 5.1 copy.67
  782.6 7.7 collective-permute-done
  (286 shorter events, 266.7 us)
Async XLA Ops:
  2.8 21.9 %all-to-all-start.1 = ((s32[32,1,2]{2,1,0:T(1,128)}), s32[32,1,2]{2,1,0:T(1,128)S(1)}, u32[]{:S(2)}, u32[]{:S(2)}) async-start(s32[32,1,2]{2,1,0:T(1,128)} %bitcast), calls=%async_computation.1 | async-start | bytes 32768 | tf_op jit(solution)/shard_map/while/body/eval_jaxpr/all_to_all | solution.py:72
  14.5 7.8 copy-start.4
  22.2 2.3 copy-start.5
  28.0 3.4 copy-start
  46.5 58.7 %all-to-all-start = ((bf16[32,2,32,512]{3,1,2,0:T(2,128)(2,1)}), bf16[32,2,32,512]{3,1,2,0:T(2,128)(2,1)}, u32[]{:S(2)}, u32[]{:S(2)}) async-start(bf16[32,2,32,512]{3,1,2,0:T(2,128)(2,1)} %copy.66), calls=%async_computation | async-start | bytes 4194304 | tf_op jit(solution)/shard_map/while/body/eval_jaxpr/all_to_all | solution.py:71
  118.0 7.7 collective-permute-start
  125.7 1.9 copy-start.1
  128.2 3.4 copy-start
  146.7 55.6 %all-to-all-start = ((bf16[32,2,32,512]{3,1,2,0:T(2,128)(2,1)}), bf16[32,2,32,512]{3,1,2,0:T(2,128)(2,1)}, u32[]{:S(2)}, u32[]{:S(2)}) async-start(bf16[32,2,32,512]{3,1,2,0:T(2,128)(2,1)} %copy.66), calls=%async_computation | async-start | bytes 4194304 | tf_op jit(solution)/shard_map/while/body/eval_jaxpr/all_to_all | solution.py:71
  215.1 7.7 collective-permute-start
  222.8 1.9 copy-start.1
  225.3 3.4 copy-start
  243.8 55.5 %all-to-all-start = ((bf16[32,2,32,512]{3,1,2,0:T(2,128)(2,1)}), bf16[32,2,32,512]{3,1,2,0:T(2,128)(2,1)}, u32[]{:S(2)}, u32[]{:S(2)}) async-start(bf16[32,2,32,512]{3,1,2,0:T(2,128)(2,1)} %copy.66), calls=%async_computation | async-start | bytes 4194304 | tf_op jit(solution)/shard_map/while/body/eval_jaxpr/all_to_all | solution.py:71
  312.1 7.7 collective-permute-start
  319.8 1.9 copy-start.1
  322.3 3.4 copy-start
  340.8 52.5 %all-to-all-start = ((bf16[32,2,32,512]{3,1,2,0:T(2,128)(2,1)}), bf16[32,2,32,512]{3,1,2,0:T(2,128)(2,1)}, u32[]{:S(2)}, u32[]{:S(2)}) async-start(bf16[32,2,32,512]{3,1,2,0:T(2,128)(2,1)} %copy.66), calls=%async_computation | async-start | bytes 4194304 | tf_op jit(solution)/shard_map/while/body/eval_jaxpr/all_to_all | solution.py:71
  406.2 7.7 collective-permute-start
  413.9 1.9 copy-start.1
  416.4 3.4 copy-start
  434.9 52.7 %all-to-all-start = ((bf16[32,2,32,512]{3,1,2,0:T(2,128)(2,1)}), bf16[32,2,32,512]{3,1,2,0:T(2,128)(2,1)}, u32[]{:S(2)}, u32[]{:S(2)}) async-start(bf16[32,2,32,512]{3,1,2,0:T(2,128)(2,1)} %copy.66), calls=%async_computation | async-start | bytes 4194304 | tf_op jit(solution)/shard_map/while/body/eval_jaxpr/all_to_all | solution.py:71
  500.4 7.7 collective-permute-start
  508.1 1.9 copy-start.1
  510.6 3.4 copy-start
  529.1 51.4 %all-to-all-start = ((bf16[32,2,32,512]{3,1,2,0:T(2,128)(2,1)}), bf16[32,2,32,512]{3,1,2,0:T(2,128)(2,1)}, u32[]{:S(2)}, u32[]{:S(2)}) async-start(bf16[32,2,32,512]{3,1,2,0:T(2,128)(2,1)} %copy.66), calls=%async_computation | async-start | bytes 4194304 | tf_op jit(solution)/shard_map/while/body/eval_jaxpr/all_to_all | solution.py:71
  593.4 7.7 collective-permute-start
  603.6 3.4 copy-start
  622.1 52.1 %all-to-all-start = ((bf16[32,2,32,512]{3,1,2,0:T(2,128)(2,1)}), bf16[32,2,32,512]{3,1,2,0:T(2,128)(2,1)}, u32[]{:S(2)}, u32[]{:S(2)}) async-start(bf16[32,2,32,512]{3,1,2,0:T(2,128)(2,1)} %copy.66), calls=%async_computation | async-start | bytes 4194304 | tf_op jit(solution)/shard_map/while/body/eval_jaxpr/all_to_all | solution.py:71
  687.0 7.7 collective-permute-start
  697.2 3.4 copy-start
  715.7 52.1 %all-to-all-start = ((bf16[32,2,32,512]{3,1,2,0:T(2,128)(2,1)}), bf16[32,2,32,512]{3,1,2,0:T(2,128)(2,1)}, u32[]{:S(2)}, u32[]{:S(2)}) async-start(bf16[32,2,32,512]{3,1,2,0:T(2,128)(2,1)} %copy.66), calls=%async_computation | async-start | bytes 4194304 | tf_op jit(solution)/shard_map/while/body/eval_jaxpr/all_to_all | solution.py:71
  780.7 9.6 %collective-permute-start = (bf16[8,32,512]{2,1,0:T(8,128)(2,1)S(1)}, bf16[8,32,512]{2,1,0:T(8,128)(2,1)S(1)}, u32[]{:S(2)}, u32[]{:S(2)}) collective-permute-start(bf16[8,32,512]{2,1,0:T(8,128)(2,1)S(1)} %get-tuple-element.515), channel_id=1, source_target_pairs={{0,32},{32,64},{64,96},{96,128},{128,160},{160,192},{192,224},{1,3... | collective-permute-start | bytes 786440 | tf_op jit(solution)/shard_map/while/body/eval_jaxpr/ppermute | solution.py:10
  (6 other events, 8.0 us)
where the time goes:
time: 795 us; the launch traced here: 791 us
  waiting for transfers between devices  424 us (53%)
  local copies, waits for them, and re-layouts  183 us (23%)
  matrix products  96.5 us (12%)
  starting transfers between devices  81 us (10%)
    all_to_all x8, waiting for transfers between devices, solve(): lax.all_to_all(outgoing, 'leaf', split_axis=0, concat_axis=0, tiled=True)  377 us
    reshape x16, local copies, waits for them, and re-layouts, solve(): outgoing.astype(jnp.bfloat16).reshape(leaf_count, bound, rows, doubled)  73.7 us
    all_to_all x8, starting transfers between devices, solve(): lax.all_to_all(outgoing, 'leaf', split_axis=0, concat_axis=0, tiled=True)  54.1 us
    ppermute x8, waiting for transfers between devices, shifted(): return lax.ppermute(value, axis, pairs)  48 us
    all_to_all x8, local copies, waits for them, and re-layouts, solve(): lax.all_to_all(outgoing, 'leaf', split_axis=0, concat_axis=0, tiled=True)  40.8 us
    reshape x8, local copies, waits for them, and re-layouts, solve(): arrived.reshape(slots, rows, doubled)  32.9 us
    dot_general x32, matrix products, complex_apply(): jnp.matmul(real_in, real_mat, preferred_element_type=jnp.float32)  24 us
    dot_general x8, matrix products, solve(): jnp.einsum('sp,prc->src', placing_half, contribution, preferred_element_t...  17.2 us
  transfers between devices with their start and end apart: 17, of which 16 were waited for; matrix products, arithmetic and copies ran while one was open for 1% of the time, Pallas kernels for 0%

commit v1 on v0

v1 whole, which is shorter than its diff:
```python
import functools

import jax
import jax.numpy as jnp
from jax import lax
from jax.experimental import pallas as pl
from jax.experimental.pallas import tpu as pltpu
from jax.sharding import PartitionSpec as P

ROWS = 4
SLOTS = 2
SKEW = 1
MESH = pl.DeviceIdType.MESH
F32 = jnp.float32
BF16 = jnp.bfloat16


def dot(a, b):
    return jnp.dot(a, b, preferred_element_type=F32)


def turned(x, rows):
    count, width = x.shape
    both = 2 * rows
    value = x.reshape(count // both, both, width)
    value = pltpu.roll(value, rows, 1)
    row = lax.broadcasted_iota(jnp.int32, value.shape, 1)
    return jnp.where(row < rows, -value, value).reshape(count, width)


def kernel(
    leafs, sweeps, rhs_ref, inc_ref, finv_hbm, coup_hbm, upd_hbm, own_ref, front_ref, out_ref,
    finv, coup, upd, comp, place, take, rhs_s, rhs_u, sol_s, contrib, field, prev, done, sent, got, told, heard,
    load_sem, prev_send, prev_recv, send_sem, recv_sem, tell_send, tell_recv,
):
    fronts, total_rows, doubled = rhs_ref.shape[1:]
    width = doubled // 2
    blocks = own_ref.shape[1]
    groups = total_rows // ROWS
    both = 2 * ROWS
    per = SLOTS * both
    pairs = fronts * blocks
    me = lax.axis_index("leaf")
    level = lax.axis_index("sweep")

    loads = [
        pltpu.make_async_copy(coup_hbm, coup, load_sem.at[0]),
        pltpu.make_async_copy(finv_hbm, finv, load_sem.at[1]),
        pltpu.make_async_copy(upd_hbm, upd, load_sem.at[2]),
    ]
    for load in loads:
        load.start()

    barrier = pltpu.get_barrier_semaphore()
    for off in range(1, leafs):
        pl.semaphore_signal(barrier, inc=1, device_id=(level, lax.rem(me + off, leafs)), device_id_type=MESH)

    @pl.when(level > 0)
    def _():
        pl.semaphore_signal(barrier, inc=1, device_id=(level - 1, me), device_id_type=MESH)

    @pl.when(level < sweeps - 1)
    def _():
        pl.semaphore_signal(barrier, inc=1, device_id=(level + 1, me), device_id_type=MESH)

    above = jnp.where(level > 0, 1, 0)
    below = jnp.where(level < sweeps - 1, 1, 0)
    pl.semaphore_wait(barrier, leafs - 1 + above + below)

    lane = lax.broadcasted_iota(jnp.int32, (fronts, pairs * both), 1)
    sub = lax.broadcasted_iota(jnp.int32, (fronts, pairs * both), 0)
    lane_front = lane // (blocks * both)
    lane_block = (lane // both) % blocks
    own = own_ref[...]
    front = front_ref[...]
    own_l = jnp.zeros_like(lane)
    front_l = jnp.zeros_like(lane)
    for k in range(blocks):
        here = (lane_block == k) & (lane_front == sub)
        own_l += jnp.where(here, own[:, k : k + 1], 0)
        front_l += jnp.where(here, front[:, k : k + 1] + 1, 0)
    own_l = jnp.sum(own_l, axis=0, keepdims=True)
    front_l = jnp.sum(front_l, axis=0, keepdims=True)
    rank = jnp.zeros_like(lane)
    for k in range(blocks):
        rank += jnp.where((own[:, k : k + 1] == own_l) & (sub < lane_front), 1, 0)
    rank = jnp.sum(rank, axis=0, keepdims=True)
    goal = (own_l * SLOTS + rank) * both + lane[:1] % both
    row = lax.broadcasted_iota(jnp.int32, (leafs * per, pairs * both), 0)
    hot = row == goal
    place[...] = jnp.where(hot, 1.0, 0.0).astype(BF16)
    labels = jnp.where(hot, front_l.astype(F32), 0.0).astype(BF16)
    told[...] = dot(labels, jnp.ones((pairs * both, 128), BF16)).astype(BF16)

    def spread(source, target, sends, recvs):
        for off in range(1, leafs):
            to = lax.rem(me + off, leafs)
            pltpu.make_async_remote_copy(
                src_ref=source.at[pl.ds(pl.multiple_of(to * per, per), per)],
                dst_ref=target.at[pl.ds(pl.multiple_of(me * per, per), per)],
                send_sem=sends,
                recv_sem=recvs,
                device_id=(level, to),
                device_id_type=MESH,
            ).start()
        mine = pl.ds(pl.multiple_of(me * per, per), per)
        target[mine, :] = source[mine, :]

    def wait_spread(ref, sem):
        part = ref.at[pl.ds(0, (leafs - 1) * per)]
        pltpu.make_async_copy(part, part, sem).wait()

    spread(told, heard, tell_send, tell_recv)

    g_row = lax.broadcasted_iota(jnp.int32, (groups * both, 2 * total_rows), 0)
    g_col = lax.broadcasted_iota(jnp.int32, (groups * both, 2 * total_rows), 1)
    from_row = ((g_row // ROWS) % 2) * total_rows + (g_row // both) * ROWS + g_row % ROWS
    regroup = jnp.where(g_col == from_row, 1.0, 0.0).astype(BF16)

    def grouped(value):
        return dot(regroup, jnp.concatenate([value[:, :width], value[:, width:]], axis=0))

    @pl.when(level == 0)
    def _():
        values = [grouped(inc_ref[i]) for i in range(fronts)]
        for g in range(groups):
            parts = [value[g * both : (g + 1) * both] for value in values]
            prev[g] = jnp.concatenate(parts, axis=0).astype(BF16)

    for load in loads:
        load.wait()

    def stacked(x):
        return jnp.concatenate([x, turned(x, ROWS)], axis=1).astype(BF16)

    def prepare(i, carry):
        value = grouped(rhs_ref[0, i])
        at_i = pl.ds(pl.multiple_of(i * both, both), both)
        for g in range(groups):
            rhs_s[g, at_i, :] = value[g * both : (g + 1) * both]
        a = finv[i].reshape(2 * width, width)
        first = stacked(dot(stacked(value), a))
        c = coup[i].reshape(2 * width, width)
        c_turned = jnp.concatenate([-c[width:], c[:width]], axis=0)
        ca = dot(jnp.concatenate([c, c_turned], axis=1), a)
        ca = ca.astype(BF16)
        ca = jnp.concatenate([ca, jnp.concatenate([-ca[width:], ca[:width]], axis=0)], axis=1)
        for k in range(blocks):
            u = upd[i, k].reshape(2 * width, width)
            comp[i, k] = dot(ca, u).astype(BF16)
            part = dot(first, u)
            at_ik = pl.ds(pl.multiple_of((i * blocks + k) * both, both), both)
            for g in range(groups):
                rhs_u[g, at_ik, :] = part[g * both : (g + 1) * both]
        return carry

    lax.fori_loop(0, fronts, prepare, 0)

    wait_spread(heard, tell_recv)
    h = heard[...].astype(F32)
    t_row = lax.broadcasted_iota(jnp.int32, h.shape, 0)
    t_lane = lax.broadcasted_iota(jnp.int32, h.shape, 1)
    fits = (h == (t_lane // both + 1).astype(F32)) & (t_row % both == t_lane % both)
    take[...] = jnp.where(fits, 1.0, 0.0).T.astype(BF16)[: fronts * both]

    def begin(g):
        @pl.when(level > 0)
        def _():
            pltpu.make_async_copy(prev.at[g], prev.at[g], prev_recv.at[g]).wait()

        x = stacked(prev[g].astype(F32))
        for i in range(fronts):
            x_i = x[i * both : (i + 1) * both]
            for k in range(blocks):
                at = (i * blocks + k) * both
                contrib[at : at + both, :] = rhs_u[g, at : at + both, :] - dot(x_i, comp[i, k])
        sent[g] = dot(place[...], contrib[...].astype(BF16)).astype(BF16)
        spread(sent.at[g], got.at[g], send_sem.at[g], recv_sem.at[g])
        for i in range(fronts):
            x_i = x[i * both : (i + 1) * both]
            at = i * both
            field[g, at : at + both, :] = rhs_s[g, at : at + both, :] - dot(x_i, coup[i].reshape(2 * width, width))

    def pass_down(g):
        return pltpu.make_async_remote_copy(
            src_ref=done.at[g],
            dst_ref=prev.at[g],
            send_sem=prev_send.at[g],
            recv_sem=prev_recv.at[g],
            device_id=(level + 1, me),
            device_id_type=MESH,
        )

    def finish(g):
        wait_spread(got.at[g], recv_sem.at[g])
        rest = field[g] - dot(take[...], got[g])
        y = stacked(rest.astype(BF16).astype(F32))
        at_g = pl.ds(pl.multiple_of(g * both, both), both)
        values = []
        for i in range(fronts):
            value = dot(y[i * both : (i + 1) * both], finv[i].reshape(2 * width, width))
            sol_s[i, at_g, :] = value
            values.append(value)
        done[g] = jnp.concatenate(values, axis=0).astype(BF16)

        @pl.when(level < sweeps - 1)
        def _():
            pass_down(g).start()

    def advance(g, carry):
        begin(g)

        @pl.when(g >= SKEW)
        def _():
            finish(g - SKEW)

        return carry

    lax.fori_loop(0, groups, advance, 0)
    for g in range(groups - SKEW, groups):
        finish(g)

    o_row = lax.broadcasted_iota(jnp.int32, (2 * total_rows, groups * both), 0)
    o_col = lax.broadcasted_iota(jnp.int32, (2 * total_rows, groups * both), 1)
    to_row = ((o_col // ROWS) % 2) * total_rows + (o_col // both) * ROWS + o_col % ROWS
    ungroup = jnp.where(o_row == to_row, 1.0, 0.0).astype(BF16)
    for i in range(fronts):
        value = dot(ungroup, sol_s[i].astype(BF16)).astype(BF16)
        out_ref[0, i, :, :width] = value[:total_rows]
        out_ref[0, i, :, width:] = value[total_rows:]

    def drain(g, carry):
        wait_spread(sent.at[g], send_sem.at[g])

        @pl.when(level < sweeps - 1)
        def _():
            pass_down(g).wait_send()

        return carry

    lax.fori_loop(0, groups, drain, 0)
    wait_spread(told, tell_send)


def body(leafs, sweeps, rhs, incoming, front_inv, coupling, update, dest_owner, dest_front):
    fronts, total_rows, doubled = incoming.shape
    width = doubled // 2
    blocks = dest_owner.shape[1]
    groups = total_rows // ROWS
    both = 2 * ROWS
    slots = leafs * SLOTS * both
    pairs = fronts * blocks
    vmem = pl.BlockSpec(memory_space=pltpu.VMEM)
    hbm = pl.BlockSpec(memory_space=pl.ANY)
    dma = pltpu.SemaphoreType.DMA
    return pl.pallas_call(
        functools.partial(kernel, leafs, sweeps),
        out_shape=jax.ShapeDtypeStruct(rhs.shape, BF16),
        in_specs=[vmem, vmem, hbm, hbm, hbm, vmem, vmem],
        out_specs=vmem,
        scratch_shapes=[
            pltpu.VMEM(front_inv.shape[1:], BF16),
            pltpu.VMEM(coupling.shape[1:], BF16),
            pltpu.VMEM(update.shape[1:], BF16),
            pltpu.VMEM((fronts, blocks, 2 * width, width), BF16),
            pltpu.VMEM((slots, pairs * both), BF16),
            pltpu.VMEM((fronts * both, slots), BF16),
            pltpu.VMEM((groups, fronts * both, width), F32),
            pltpu.VMEM((groups, pairs * both, width), F32),
            pltpu.VMEM((fronts, groups * both, width), F32),
            pltpu.VMEM((pairs * both, width), F32),
            pltpu.VMEM((groups, fronts * both, width), F32),
            pltpu.VMEM((groups, fronts * both, width), BF16),
            pltpu.VMEM((groups, fronts * both, width), BF16),
            pltpu.VMEM((groups, slots, width), BF16),
            pltpu.VMEM((groups, slots, width), BF16),
            pltpu.VMEM((slots, 128), BF16),
            pltpu.VMEM((slots, 128), BF16),
            dma((3,)),
            dma((groups,)),
            dma((groups,)),
            dma((groups,)),
            dma((groups,)),
            dma,
            dma,
        ],
        compiler_params=pltpu.CompilerParams(
            collective_id=0, has_side_effects=True, vmem_limit_bytes=60 * 1024 * 1024
        ),
    )(rhs, incoming, front_inv[0], coupling[0], update[0], dest_owner, dest_front)


def solution(mesh):
    return jax.shard_map(
        functools.partial(body, mesh.shape["leaf"], mesh.shape["sweep"]),
        mesh=mesh,
        in_specs=(
            P("sweep", "leaf", None, None),
            P("leaf", None, None),
            P("sweep", "leaf", None, None, None),
            P("sweep", "leaf", None, None, None),
            P("sweep", "leaf", None, None, None, None),
            P("leaf", None),
            P("leaf", None),
        ),
        out_specs=P("sweep", "leaf", None, None),
        check_vma=False,
    )
```

time: 795 us -> 170 us (0.21)
  the two profiles are of different devices: /device:TPU:10 before, /device:TPU:25 now
where the time goes in v1:
time: 170 us; the launch traced here: 169 us
  Pallas kernels  165 us (97%)
  local copies, waits for them, and re-layouts  4.36 us (3%)
    pallas_call x1, Pallas kernels, body(): pl.pallas_call(functools.partial(kernel, leafs, sweeps), out_shape=jax.Sh...  165 us
    unnamed x3, local copies, waits for them, and re-layouts  4.36 us

profile of v1, /device:TPU:25, one launch (start us, length us, event | category | flops | bytes accessed | tf_op | source)
XLA Modules:
  0.0 169.5 jit_solution(8589574265450540305)
XLA Ops:
  0.0 1.3 copy.8.own_ref
  1.3 1.3 copy.9.front_ref
  2.7 165.1 %shard_map.73 = bf16[1,8,32,512]{3,2,1,0:T(8,128)(2,1)} custom-call(bf16[1,8,32,512]{3,2,1,0:T(8,128)(2,1)} %rhs_ref.1, bf16[8,32,512]{2,1,0:T(8,128)(2,1)} %inc_ref.1, bf16[8,2,256,256]{3,2,1,0:T(8,128)(2,1)} %bitcast.4, bf16[8,2,256,256]{3,2,1,0:T(8,128)(2,1)} %bitcast.5, bf16[8,4,2,256,256]{4,3,2,1,0:T(8,128)(2,1)} %bitcast.3, s32[8,4]{1,0:T(8,128)} %copy.8.own_ref, ...), custom_call_target="tpu_custom_call" | custom-call | tf_op jit(solution)/shard_map/pallas_call | solution.py:256
  167.8 1.7 copy.11

commit v2 on v1

v2 whole, which is shorter than its diff:
```python
import functools

import jax
import jax.numpy as jnp
from jax import lax
from jax.experimental import pallas as pl
from jax.experimental.pallas import tpu as pltpu
from jax.sharding import PartitionSpec as P

ROWS = 2
SLOTS = 2
LANES = 128
TOGETHER = 2
LEAF_X = 4
UNIT = 8
PER = SLOTS * UNIT
SKEW = 3
MESH = pl.DeviceIdType.MESH
F32 = jnp.float32
BF16 = jnp.bfloat16


def dot(a, b):
    return jnp.dot(a, b, preferred_element_type=F32)


def expand(v):
    a = v.reshape(v.shape[0] // UNIT, UNIT, LANES)
    b = pltpu.roll(a, UNIT // 2, 1)
    row = lax.broadcasted_iota(jnp.int32, a.shape, 1)
    first = jnp.where(row < UNIT // 2, a, b)
    second = jnp.where(row < UNIT // 2, b, a)
    real = row % (UNIT // 2) < ROWS
    parts = [first, second]
    for half in (first, second):
        swapped = pltpu.roll(half, ROWS, 1)
        parts.append(jnp.where(real, -swapped, swapped))
    return jnp.concatenate(parts, axis=2).reshape(v.shape[0], 4 * LANES).astype(BF16)


def collapse(p):
    a = p.reshape(p.shape[0] // UNIT, UNIT, 2 * LANES)
    row = lax.broadcasted_iota(jnp.int32, (a.shape[0], UNIT, LANES), 1)
    return jnp.where(row < UNIT // 2, a[:, :, :LANES], a[:, :, LANES:]).reshape(p.shape[0], LANES)


def beside(m):
    half = m.shape[0] // 2
    return jnp.concatenate([m, jnp.concatenate([-m[half:], m[:half]], axis=0)], axis=1)


def kernel(
    leafs, sweeps, rhs_ref, inc_ref, finv_hbm, coup_hbm, upd_hbm, own_ref, front_ref, out_ref,
    finv, coup, upd, above, comp_d, comp_u, place, take, rhs_s, rhs_u, contrib, rest, back, above_field,
    sent, got, last, told, heard,
    load_sem, above_send, above_recv, field_send, field_recv, back_send, back_recv, sent_sem, got_sem, last_sem,
    told_sem, heard_sem,
):
    fronts, total_rows, doubled = rhs_ref.shape[1:]
    width = doubled // 2
    blocks = own_ref.shape[0]
    groups = total_rows // ROWS
    pairs = fronts * blocks
    top = sweeps - 1
    me = lax.axis_index("leaf")
    level = lax.axis_index("sweep")

    def load(which, i):
        source, target = ((finv_hbm, finv), (coup_hbm, coup), (upd_hbm, upd))[which]
        return pltpu.make_async_copy(source.at[i], target.at[i], load_sem.at[which, i])

    for i in range(fronts):
        load(0, i).start()
    for i in range(fronts):
        load(1, i).start()
        load(2, i).start()

    barrier = pltpu.get_barrier_semaphore()

    @pl.when(level > 0)
    def _():
        for to in range(leafs):
            pl.semaphore_signal(barrier, inc=1, device_id=(level - 1, to), device_id_type=MESH)

    @pl.when(level < top)
    def _():
        pl.semaphore_signal(barrier, inc=1, device_id=(level + 1, me), device_id_type=MESH)

    @pl.when(level == top)
    def _():
        for off in range(1, leafs):
            pl.semaphore_signal(barrier, inc=1, device_id=(level, lax.rem(me + off, leafs)), device_id_type=MESH)

    lane = lax.broadcasted_iota(jnp.int32, (fronts, pairs * UNIT), 1)
    sub = lax.broadcasted_iota(jnp.int32, (fronts, pairs * UNIT), 0)
    lane_front = lane // (blocks * UNIT)
    lane_block = (lane // UNIT) % blocks
    own = own_ref[...].T
    front = front_ref[...].T
    own_l = jnp.zeros_like(lane)
    front_l = jnp.zeros_like(lane)
    for k in range(blocks):
        here = (lane_block == k) & (lane_front == sub)
        own_l += jnp.where(here, own[:, k : k + 1], 0)
        front_l += jnp.where(here, front[:, k : k + 1] + 1, 0)
    own_l = jnp.sum(own_l, axis=0, keepdims=True)
    front_l = jnp.sum(front_l, axis=0, keepdims=True)
    rank = jnp.zeros_like(lane)
    for k in range(blocks):
        rank += jnp.where((own[:, k : k + 1] == own_l) & (sub < lane_front), 1, 0)
    rank = jnp.sum(rank, axis=0, keepdims=True)
    goal = (own_l * SLOTS + rank) * UNIT + lane[:1] % UNIT
    row = lax.broadcasted_iota(jnp.int32, (leafs * PER, pairs * UNIT), 0)
    hot = row == goal
    place[...] = jnp.where(hot, 1.0, 0.0).astype(BF16)
    labels = jnp.where(hot, front_l.astype(F32), 0.0).astype(BF16)
    told[...] = dot(labels, jnp.ones((pairs * UNIT, LANES), BF16)).astype(BF16)

    waits = jnp.where(level < top, leafs, leafs - 1) + jnp.where(level > 0, 1, 0)
    pl.semaphore_wait(barrier, waits)

    leaf_z = leafs // LEAF_X
    steps = [(dz, dx) for dz in range(leaf_z) for dx in range(LEAF_X)]
    steps.sort(key=lambda d: -min(d[0], leaf_z - d[0]) - min(d[1], LEAF_X - d[1]))

    mine = pl.ds(pl.multiple_of(me * PER, PER), PER)

    def spread(source, target, sends, recvs, to_level, offsets):
        for dz, dx in offsets:
            to = lax.rem(me // LEAF_X + dz, leaf_z) * LEAF_X + lax.rem(me % LEAF_X + dx, LEAF_X)
            pltpu.make_async_remote_copy(
                src_ref=source.at[pl.ds(pl.multiple_of(to * PER, PER), PER)],
                dst_ref=target.at[mine],
                send_sem=sends,
                recv_sem=recvs,
                device_id=(to_level, to),
                device_id_type=MESH,
            ).start()

    def wait_for(ref, sem):
        pltpu.make_async_copy(ref, ref, sem).wait()

    def others(ref):
        return ref.at[pl.ds(0, (leafs - 1) * PER)]

    def hand(source, target, send, recv, to_level):
        return pltpu.make_async_remote_copy(
            src_ref=source,
            dst_ref=target,
            send_sem=send,
            recv_sem=recv,
            device_id=(to_level, me),
            device_id_type=MESH,
        )

    def hand_inverse(i):
        return hand(finv_hbm.at[i], above.at[i], above_send.at[i], above_recv.at[i], level + 1)

    def hand_field(g):
        return hand(rhs_s.at[g], above_field.at[g], field_send.at[g], field_recv.at[g], level + 1)

    def hand_back(g):
        return hand(rest.at[g], back.at[g], back_send.at[g], back_recv.at[g], level - 1)

    @pl.when(level < top)
    def _():
        for i in range(fronts):
            hand_inverse(i).start()
        spread(told, heard, told_sem, heard_sem, level + 1, steps)

    def packed_place(index):
        at = (index // ROWS) % 2 * 2 + (index // (2 * ROWS)) % 2
        return at * total_rows + (index // UNIT) * ROWS + index % ROWS

    spots = groups * UNIT
    square_row = lax.broadcasted_iota(jnp.int32, (spots, spots), 0)
    square_col = lax.broadcasted_iota(jnp.int32, (spots, spots), 1)

    def packed(value):
        regroup = jnp.where(square_col == packed_place(square_row), 1.0, 0.0).astype(BF16)
        parts = [value[:, t * LANES : (t + 1) * LANES] for t in range(doubled // LANES)]
        return dot(regroup, jnp.concatenate(parts, axis=0))

    def apply(v, m):
        return collapse(dot(expand(v), m))

    def flat(ref, *at):
        return ref[at].reshape(2 * width, width)

    def rounded(v):
        return v.astype(BF16).astype(F32)

    starts = jnp.where(level == 0, 1.0, 0.0).astype(F32)

    def begin(b, carry):
        these = [b * TOGETHER + n for n in range(TOGETHER)]
        for i in these:
            for which in range(3):
                load(which, i).wait()
        entering = [expand(packed(inc_ref[i])) for i in these]
        fields = [packed(rhs_ref[0, i]) for i in these]
        fields = [
            field - starts * collapse(dot(x, flat(coup, i))) for i, x, field in zip(these, entering, fields)
        ]
        firsts = [expand(rounded(apply(rounded(field), flat(finv, i)))) for i, field in zip(these, fields)]
        for i, field in zip(these, fields):
            at_i = pl.ds(pl.multiple_of(i * UNIT, UNIT), UNIT)
            for g in range(groups):
                rhs_s[g, at_i, :] = field[g * UNIT : (g + 1) * UNIT]
        for i, first in zip(these, firsts):
            for k in range(blocks):
                part = collapse(dot(first, flat(upd, i, k)))
                at_ik = pl.ds(pl.multiple_of((i * blocks + k) * UNIT, UNIT), UNIT)
                for g in range(groups):
                    rhs_u[g, at_ik, :] = part[g * UNIT : (g + 1) * UNIT]
        return carry

    lax.fori_loop(0, fronts // TOGETHER, begin, 0)

    def compose(i, carry):
        wait_for(above.at[i], above_recv.at[i])
        d = dot(beside(flat(above, i)), flat(coup, i)).astype(BF16)
        comp_d[i] = d
        e = beside(dot(beside(d), flat(finv, i)).astype(BF16))
        for k in range(blocks):
            comp_u[i, :, k * width : (k + 1) * width] = dot(e, flat(upd, i, k)).astype(BF16)
        return carry

    @pl.when(level > 0)
    def _():
        lax.fori_loop(0, fronts, compose, 0)

    @pl.when(level > 0)
    def _():
        wait_for(heard, heard_sem)
        h = heard[...].astype(F32)
        t_row = lax.broadcasted_iota(jnp.int32, h.shape, 0)
        t_lane = lax.broadcasted_iota(jnp.int32, h.shape, 1)
        fits = (h == (t_lane // UNIT + 1).astype(F32)) & (t_row % UNIT == t_lane % UNIT)
        take[...] = jnp.where(fits, 1.0, 0.0).T.astype(BF16)[: fronts * UNIT]

    def step(g):
        @pl.when(level == 0)
        def _():
            contrib[...] = rhs_u[g].astype(BF16)

        @pl.when(level > 0)
        def _():
            wait_for(above_field.at[g], field_recv.at[g])
            wait_for(got.at[g], got_sem.at[g])
            rest[g] = (above_field[g] - dot(take[...], got[g])).astype(BF16)
            hand_back(g).start()
            x = expand(rest[g].astype(F32))
            values = []
            for i in range(fronts):
                wide = dot(x[i * UNIT : (i + 1) * UNIT], comp_u[i])
                for k in range(blocks):
                    at = (i * blocks + k) * UNIT
                    values.append(rhs_u[g, at : at + UNIT, :] - collapse(wide[:, k * width : (k + 1) * width]))
            contrib[...] = jnp.concatenate(values, axis=0).astype(BF16)

        sent[g] = dot(place[...], contrib[...]).astype(BF16)

        @pl.when(level < top)
        def _():
            spread(sent.at[g], got.at[g], sent_sem.at[g], got_sem.at[g], level + 1, steps)

        @pl.when(level == top)
        def _():
            spread(sent.at[g], last.at[g], sent_sem.at[g], last_sem.at[g], level, steps[:-1])
            last[g, mine, :] = sent[g, mine, :]

        @pl.when(level > 0)
        def _():
            x = expand(rest[g].astype(F32))
            for i in range(fronts):
                at = i * UNIT
                value = collapse(dot(x[at : at + UNIT], comp_d[i]))
                rhs_s[g, at : at + UNIT, :] = rhs_s[g, at : at + UNIT, :] - value

        @pl.when(level < top)
        def _():
            hand_field(g).start()

    def close(g):
        wait_for(others(last.at[g]), last_sem.at[g])
        back[g] = (rhs_s[g] - dot(take[...], last[g])).astype(BF16)

    def advance(g, carry):
        step(g)

        @pl.when((level == top) & (g >= SKEW))
        def _():
            close(g - SKEW)

        return carry

    lax.fori_loop(0, groups, advance, 0)

    @pl.when(level == top)
    def _():
        for g in range(groups - SKEW, groups):
            close(g)

    @pl.when(level < top)
    def _():
        for g in range(groups):
            wait_for(back.at[g], back_recv.at[g])

    ungroup = jnp.where(square_row == packed_place(square_col), 1.0, 0.0).astype(BF16)
    for i in range(fronts):
        at = i * UNIT
        value = jnp.concatenate([back[g].astype(F32)[at : at + UNIT] for g in range(groups)], axis=0)
        solved = apply(value, flat(finv, i)).astype(BF16)
        value = dot(ungroup, solved).astype(BF16)
        for t in range(doubled // LANES):
            out_ref[0, i, :, t * LANES : (t + 1) * LANES] = value[t * total_rows : (t + 1) * total_rows]

    @pl.when(level < top)
    def _():
        wait_for(told, told_sem)
        for i in range(fronts):
            hand_inverse(i).wait_send()

        def drain(g, carry):
            wait_for(sent.at[g], sent_sem.at[g])
            hand_field(g).wait_send()
            return carry

        lax.fori_loop(0, groups, drain, 0)

    @pl.when(level > 0)
    def _():
        def drain(g, carry):
            hand_back(g).wait_send()
            return carry

        lax.fori_loop(0, groups, drain, 0)

    @pl.when(level == top)
    def _():
        def drain(g, carry):
            wait_for(others(sent.at[g]), sent_sem.at[g])
            return carry

        lax.fori_loop(0, groups, drain, 0)


def body(leafs, sweeps, rhs, incoming, front_inv, coupling, update, dest_owner, dest_front):
    fronts, total_rows, doubled = incoming.shape
    width = doubled // 2
    blocks = dest_owner.shape[1]
    groups = total_rows // ROWS
    slots = leafs * PER
    pairs = fronts * blocks
    vmem = pl.BlockSpec(memory_space=pltpu.VMEM)
    hbm = pl.BlockSpec(memory_space=pl.ANY)
    dma = pltpu.SemaphoreType.DMA
    return pl.pallas_call(
        functools.partial(kernel, leafs, sweeps),
        out_shape=jax.ShapeDtypeStruct(rhs.shape, BF16),
        in_specs=[vmem, vmem, hbm, hbm, hbm, vmem, vmem],
        out_specs=vmem,
        scratch_shapes=[
            pltpu.VMEM(front_inv.shape[1:], BF16),
            pltpu.VMEM(coupling.shape[1:], BF16),
            pltpu.VMEM(update.shape[1:], BF16),
            pltpu.VMEM(front_inv.shape[1:], BF16),
            pltpu.VMEM((fronts, 2 * width, width), BF16),
            pltpu.VMEM((fronts, 2 * width, blocks * width), BF16),
            pltpu.VMEM((slots, pairs * UNIT), BF16),
            pltpu.VMEM((fronts * UNIT, slots), BF16),
            pltpu.VMEM((groups, fronts * UNIT, LANES), F32),
            pltpu.VMEM((groups, pairs * UNIT, LANES), F32),
            pltpu.VMEM((pairs * UNIT, LANES), BF16),
            pltpu.VMEM((groups, fronts * UNIT, LANES), BF16),
            pltpu.VMEM((groups, fronts * UNIT, LANES), BF16),
            pltpu.VMEM((groups, fronts * UNIT, LANES), F32),
            pltpu.VMEM((groups, slots, LANES), BF16),
            pltpu.VMEM((groups, slots, LANES), BF16),
            pltpu.VMEM((groups, slots, LANES), BF16),
            pltpu.VMEM((slots, LANES), BF16),
            pltpu.VMEM((slots, LANES), BF16),
            dma((3, fronts)),
            dma((fronts,)),
            dma((fronts,)),
            dma((groups,)),
            dma((groups,)),
            dma((groups,)),
            dma((groups,)),
            dma((groups,)),
            dma((groups,)),
            dma((groups,)),
            dma,
            dma,
        ],
        compiler_params=pltpu.CompilerParams(
            collective_id=0, has_side_effects=True, vmem_limit_bytes=60 * 1024 * 1024
        ),
    )(rhs, incoming, front_inv[0], coupling[0], update[0], dest_owner.T, dest_front.T)


def solution(mesh):
    return jax.shard_map(
        functools.partial(body, mesh.shape["leaf"], mesh.shape["sweep"]),
        mesh=mesh,
        in_specs=(
            P("sweep", "leaf", None, None),
            P("leaf", None, None),
            P("sweep", "leaf", None, None, None),
            P("sweep", "leaf", None, None, None),
            P("sweep", "leaf", None, None, None, None),
            P("leaf", None),
            P("leaf", None),
        ),
        out_specs=P("sweep", "leaf", None, None),
        check_vma=False,
    )
```

time: 170 us -> 138 us (0.81)
  Pallas kernels: 165 us -> 136 us
  local copies, waits for them, and re-layouts: 4.36 us -> 1.67 us
    pallas_call x1, Pallas kernels: 165 us -> 136 us  [body(): pl.pallas_call(functools.partial(kernel, leafs, sweeps), out_shape=jax.Sh...]
    unnamed x3 -> x1, local copies, waits for them, and re-layouts: 4.36 us -> 1.67 us
where the time goes in v2:
time: 138 us
  Pallas kernels  136 us (99%)
  local copies, waits for them, and re-layouts  1.67 us (1%)
    pallas_call x1, Pallas kernels, body(): pl.pallas_call(functools.partial(kernel, leafs, sweeps), out_shape=jax.Sh...  136 us

profile of v2, /device:TPU:25, one launch (start us, length us, event | category | flops | bytes accessed | tf_op | source)
XLA Modules:
  0.0 137.7 jit_solution(1720839829666414876)
XLA Ops:
  0.0 136.0 %shard_map.73 = bf16[1,8,32,512]{3,2,1,0:T(8,128)(2,1)} custom-call(bf16[1,8,32,512]{3,2,1,0:T(8,128)(2,1)} %rhs_ref.1, bf16[8,32,512]{2,1,0:T(8,128)(2,1)} %inc_ref.1, bf16[8,2,256,256]{3,2,1,0:T(8,128)(2,1)} %bitcast.6, bf16[8,2,256,256]{3,2,1,0:T(8,128)(2,1)} %bitcast.7, bf16[8,4,2,256,256]{4,3,2,1,0:T(8,128)(2,1)} %bitcast.5, s32[4,8]{1,0:T(4,128)} %bitcast.8, ...), custom_call_target="tpu_custom_call" | custom-call | tf_op jit(solution)/shard_map/pallas_call | solution.py:359
  136.0 1.7 %copy.9 = bf16[1,8,32,512]{3,2,1,0:T(8,128)(2,1)} copy(bf16[1,8,32,512]{3,2,1,0:T(8,128)(2,1)} %shard_map.73) | data formatting | bytes 524288

commit v3 on v2

--- a/solution.py
+++ b/solution.py
@@ -10,11 +10,12 @@
 ROWS = 2
 SLOTS = 2
 LANES = 128
-TOGETHER = 2
+TOGETHER = 4
 LEAF_X = 4
 UNIT = 8
 PER = SLOTS * UNIT
-SKEW = 3
+SKEW = 2
+HANDED = 1
 MESH = pl.DeviceIdType.MESH
 F32 = jnp.float32
 BF16 = jnp.bfloat16
@@ -52,8 +53,8 @@
 def kernel(
     leafs, sweeps, rhs_ref, inc_ref, finv_hbm, coup_hbm, upd_hbm, own_ref, front_ref, out_ref,
     finv, coup, upd, above, comp_d, comp_u, place, take, rhs_s, rhs_u, contrib, rest, back, above_field,
-    sent, got, last, told, heard,
-    load_sem, above_send, above_recv, field_send, field_recv, back_send, back_recv, sent_sem, got_sem, last_sem,
+    result, solved, entered, sent, got, last, told, heard,
+    load_sem, above_send, above_recv, field_send, field_recv, back_send, back_recv, solved_send, entered_recv, sent_sem, got_sem, last_sem,
     told_sem, heard_sem,
 ):
     fronts, total_rows, doubled = rhs_ref.shape[1:]
@@ -64,6 +65,9 @@
     top = sweeps - 1
     me = lax.axis_index("leaf")
     level = lax.axis_index("sweep")
+    kept = (level == HANDED) | (level == top)
+    entry = level == HANDED + 1
+    fused = (level > 0) & (level != HANDED + 1)
 
     def load(which, i):
         source, target = ((finv_hbm, finv), (coup_hbm, coup), (upd_hbm, upd))[which]
@@ -77,16 +81,20 @@
 
     barrier = pltpu.get_barrier_semaphore()
 
-    @pl.when(level > 0)
+    @pl.when(fused)
     def _():
         for to in range(leafs):
             pl.semaphore_signal(barrier, inc=1, device_id=(level - 1, to), device_id_type=MESH)
 
-    @pl.when(level < top)
+    @pl.when(entry)
+    def _():
+        pl.semaphore_signal(barrier, inc=1, device_id=(level - 1, me), device_id_type=MESH)
+
+    @pl.when(jnp.logical_not(kept))
     def _():
         pl.semaphore_signal(barrier, inc=1, device_id=(level + 1, me), device_id_type=MESH)
 
-    @pl.when(level == top)
+    @pl.when(kept)
     def _():
         for off in range(1, leafs):
             pl.semaphore_signal(barrier, inc=1, device_id=(level, lax.rem(me + off, leafs)), device_id_type=MESH)
@@ -116,7 +124,7 @@
     labels = jnp.where(hot, front_l.astype(F32), 0.0).astype(BF16)
     told[...] = dot(labels, jnp.ones((pairs * UNIT, LANES), BF16)).astype(BF16)
 
-    waits = jnp.where(level < top, leafs, leafs - 1) + jnp.where(level > 0, 1, 0)
+    waits = jnp.where(kept, leafs - 1, leafs) + jnp.where(fused, 1, 0) + jnp.where(level == HANDED, 1, 0)
     pl.semaphore_wait(barrier, waits)
 
     leaf_z = leafs // LEAF_X
@@ -159,10 +167,13 @@
     def hand_field(g):
         return hand(rhs_s.at[g], above_field.at[g], field_send.at[g], field_recv.at[g], level + 1)
 
+    def hand_solved(g):
+        return hand(solved.at[g], entered.at[g], solved_send.at[g], entered_recv.at[g], level + 1)
+
     def hand_back(g):
         return hand(rest.at[g], back.at[g], back_send.at[g], back_recv.at[g], level - 1)
 
-    @pl.when(level < top)
+    @pl.when(jnp.logical_not(kept))
     def _():
         for i in range(fronts):
             hand_inverse(i).start()
@@ -217,20 +228,34 @@
 
     lax.fori_loop(0, fronts // TOGETHER, begin, 0)
 
-    def compose(i, carry):
-        wait_for(above.at[i], above_recv.at[i])
-        d = dot(beside(flat(above, i)), flat(coup, i)).astype(BF16)
-        comp_d[i] = d
-        e = beside(dot(beside(d), flat(finv, i)).astype(BF16))
+    def compose(b, carry):
+        these = [b * TOGETHER + n for n in range(TOGETHER)]
+        for i in these:
+            @pl.when(fused)
+            def _():
+                wait_for(above.at[i], above_recv.at[i])
+
+            @pl.when(entry)
+            def _():
+                unit_row = lax.broadcasted_iota(jnp.int32, (width, width), 0)
+                unit_col = lax.broadcasted_iota(jnp.int32, (width, width), 1)
+                above[i, 0] = jnp.where(unit_row == unit_col, 1.0, 0.0).astype(BF16)
+                above[i, 1] = jnp.zeros((width, width), BF16)
+
+        downs = [dot(beside(flat(above, i)), flat(coup, i)).astype(BF16) for i in these]
+        for i, down in zip(these, downs):
+            comp_d[i] = down
+        firsts = [beside(dot(beside(down), flat(finv, i)).astype(BF16)) for i, down in zip(these, downs)]
         for k in range(blocks):
-            comp_u[i, :, k * width : (k + 1) * width] = dot(e, flat(upd, i, k)).astype(BF16)
+            for i, first in zip(these, firsts):
+                comp_u[i, :, k * width : (k + 1) * width] = dot(first, flat(upd, i, k)).astype(BF16)
         return carry
 
     @pl.when(level > 0)
     def _():
-        lax.fori_loop(0, fronts, compose, 0)
-
-    @pl.when(level > 0)
+        lax.fori_loop(0, fronts // TOGETHER, compose, 0)
+
+    @pl.when(fused)
     def _():
         wait_for(heard, heard_sem)
         h = heard[...].astype(F32)
@@ -246,10 +271,18 @@
 
         @pl.when(level > 0)
         def _():
-            wait_for(above_field.at[g], field_recv.at[g])
-            wait_for(got.at[g], got_sem.at[g])
-            rest[g] = (above_field[g] - dot(take[...], got[g])).astype(BF16)
-            hand_back(g).start()
+            @pl.when(fused)
+            def _():
+                wait_for(above_field.at[g], field_recv.at[g])
+                wait_for(got.at[g], got_sem.at[g])
+                rest[g] = (above_field[g] - dot(take[...], got[g])).astype(BF16)
+                hand_back(g).start()
+
+            @pl.when(entry)
+            def _():
+                wait_for(entered.at[g], entered_recv.at[g])
+                rest[g] = entered[g]
+
             x = expand(rest[g].astype(F32))
             values = []
             for i in range(fronts):
@@ -261,11 +294,11 @@
 
         sent[g] = dot(place[...], contrib[...]).astype(BF16)
 
-        @pl.when(level < top)
+        @pl.when(jnp.logical_not(kept))
         def _():
             spread(sent.at[g], got.at[g], sent_sem.at[g], got_sem.at[g], level + 1, steps)
 
-        @pl.when(level == top)
+        @pl.when(kept)
         def _():
             spread(sent.at[g], last.at[g], sent_sem.at[g], last_sem.at[g], level, steps[:-1])
             last[g, mine, :] = sent[g, mine, :]
@@ -278,18 +311,30 @@
                 value = collapse(dot(x[at : at + UNIT], comp_d[i]))
                 rhs_s[g, at : at + UNIT, :] = rhs_s[g, at : at + UNIT, :] - value
 
-        @pl.when(level < top)
+        @pl.when(jnp.logical_not(kept))
         def _():
             hand_field(g).start()
 
     def close(g):
         wait_for(others(last.at[g]), last_sem.at[g])
-        back[g] = (rhs_s[g] - dot(take[...], last[g])).astype(BF16)
+        value = (rhs_s[g] - dot(take[...], last[g])).astype(BF16)
+        x = expand(value.astype(F32))
+        at_g = pl.ds(pl.multiple_of(g * UNIT, UNIT), UNIT)
+        values = []
+        for i in range(fronts):
+            value = collapse(dot(x[i * UNIT : (i + 1) * UNIT], flat(finv, i)))
+            result[i, at_g, :] = value
+            values.append(value)
+
+        @pl.when(level == HANDED)
+        def _():
+            solved[g] = jnp.concatenate(values, axis=0).astype(BF16)
+            hand_solved(g).start()
 
     def advance(g, carry):
         step(g)
 
-        @pl.when((level == top) & (g >= SKEW))
+        @pl.when(kept & (g >= SKEW))
         def _():
             close(g - SKEW)
 
@@ -297,26 +342,30 @@
 
     lax.fori_loop(0, groups, advance, 0)
 
-    @pl.when(level == top)
-    def _():
-        for g in range(groups - SKEW, groups):
+    @pl.when(kept)
+    def _():
+        def finish(g, carry):
             close(g)
-
-    @pl.when(level < top)
+            return carry
+
+        lax.fori_loop(groups - SKEW, groups, finish, 0)
+
+    @pl.when(jnp.logical_not(kept))
     def _():
         for g in range(groups):
             wait_for(back.at[g], back_recv.at[g])
+        for i in range(fronts):
+            at = i * UNIT
+            value = jnp.concatenate([back[g].astype(F32)[at : at + UNIT] for g in range(groups)], axis=0)
+            result[i] = apply(value, flat(finv, i))
 
     ungroup = jnp.where(square_row == packed_place(square_col), 1.0, 0.0).astype(BF16)
     for i in range(fronts):
-        at = i * UNIT
-        value = jnp.concatenate([back[g].astype(F32)[at : at + UNIT] for g in range(groups)], axis=0)
-        solved = apply(value, flat(finv, i)).astype(BF16)
-        value = dot(ungroup, solved).astype(BF16)
+        value = dot(ungroup, result[i].astype(BF16)).astype(BF16)
         for t in range(doubled // LANES):
             out_ref[0, i, :, t * LANES : (t + 1) * LANES] = value[t * total_rows : (t + 1) * total_rows]
 
-    @pl.when(level < top)
+    @pl.when(jnp.logical_not(kept))
     def _():
         wait_for(told, told_sem)
         for i in range(fronts):
@@ -329,7 +378,7 @@
 
         lax.fori_loop(0, groups, drain, 0)
 
-    @pl.when(level > 0)
+    @pl.when(fused)
     def _():
         def drain(g, carry):
             hand_back(g).wait_send()
@@ -337,10 +386,18 @@
 
         lax.fori_loop(0, groups, drain, 0)
 
-    @pl.when(level == top)
+    @pl.when(kept)
     def _():
         def drain(g, carry):
             wait_for(others(sent.at[g]), sent_sem.at[g])
+            return carry
+
+        lax.fori_loop(0, groups, drain, 0)
+
+    @pl.when(level == HANDED)
+    def _():
+        def drain(g, carry):
+            hand_solved(g).wait_send()
             return carry
 
         lax.fori_loop(0, groups, drain, 0)
@@ -376,6 +433,9 @@
             pltpu.VMEM((groups, fronts * UNIT, LANES), BF16),
             pltpu.VMEM((groups, fronts * UNIT, LANES), BF16),
             pltpu.VMEM((groups, fronts * UNIT, LANES), F32),
+            pltpu.VMEM((fronts, groups * UNIT, LANES), F32),
+            pltpu.VMEM((groups, fronts * UNIT, LANES), BF16),
+            pltpu.VMEM((groups, fronts * UNIT, LANES), BF16),
             pltpu.VMEM((groups, slots, LANES), BF16),
             pltpu.VMEM((groups, slots, LANES), BF16),
             pltpu.VMEM((groups, slots, LANES), BF16),
@@ -384,6 +444,8 @@
             dma((3, fronts)),
             dma((fronts,)),
             dma((fronts,)),
+            dma((groups,)),
+            dma((groups,)),
             dma((groups,)),
             dma((groups,)),
             dma((groups,)),

time: 138 us -> 122 us (0.88)
  Pallas kernels: 136 us -> 120 us
    pallas_call x1, Pallas kernels: 136 us -> 120 us  [body(): pl.pallas_call(functools.partial(kernel, leafs, sweeps), out_shape=jax.Sh...]
where the time goes in v3:
time: 122 us
  Pallas kernels  120 us (98%)
  local copies, waits for them, and re-layouts  1.67 us (1%)
    pallas_call x1, Pallas kernels, body(): pl.pallas_call(functools.partial(kernel, leafs, sweeps), out_shape=jax.Sh...  120 us

profile of v3, /device:TPU:25, one launch (start us, length us, event | category | flops | bytes accessed | tf_op | source)
XLA Modules:
  0.0 121.8 jit_solution(1558626239337899389)
XLA Ops:
  0.0 120.2 %shard_map.73 = bf16[1,8,32,512]{3,2,1,0:T(8,128)(2,1)} custom-call(bf16[1,8,32,512]{3,2,1,0:T(8,128)(2,1)} %rhs_ref.1, bf16[8,32,512]{2,1,0:T(8,128)(2,1)} %inc_ref.1, bf16[8,2,256,256]{3,2,1,0:T(8,128)(2,1)} %bitcast.6, bf16[8,2,256,256]{3,2,1,0:T(8,128)(2,1)} %bitcast.7, bf16[8,4,2,256,256]{4,3,2,1,0:T(8,128)(2,1)} %bitcast.5, s32[4,8]{1,0:T(4,128)} %bitcast.8, ...), custom_call_target="tpu_custom_call" | custom-call | tf_op jit(solution)/shard_map/pallas_call | solution.py:416
  120.2 1.7 %copy.9 = bf16[1,8,32,512]{3,2,1,0:T(8,128)(2,1)} copy(bf16[1,8,32,512]{3,2,1,0:T(8,128)(2,1)} %shard_map.73) | data formatting | bytes 524288

commit v4 on v3

--- a/solution.py
+++ b/solution.py
@@ -15,6 +15,7 @@
 UNIT = 8
 PER = SLOTS * UNIT
 SKEW = 2
+WINDOW = 4
 HANDED = 1
 MESH = pl.DeviceIdType.MESH
 F32 = jnp.float32
@@ -51,13 +52,13 @@
 
 
 def kernel(
-    leafs, sweeps, rhs_ref, inc_ref, finv_hbm, coup_hbm, upd_hbm, own_ref, front_ref, out_ref,
-    finv, coup, upd, above, comp_d, comp_u, place, take, rhs_s, rhs_u, contrib, rest, back, above_field,
+    leafs, sweeps, rhs_hbm, inc_hbm, finv_hbm, coup_hbm, upd_hbm, own_ref, front_ref, out_ref,
+    rhs_ref, inc_ref, finv, coup, upd, above, comp_d, comp_u, place, take, rhs_s, rhs_u, rest, back, above_field,
     result, solved, entered, sent, got, last, told, heard,
     load_sem, above_send, above_recv, field_send, field_recv, back_send, back_recv, solved_send, entered_recv, sent_sem, got_sem, last_sem,
     told_sem, heard_sem,
 ):
-    fronts, total_rows, doubled = rhs_ref.shape[1:]
+    fronts, total_rows, doubled = inc_ref.shape
     width = doubled // 2
     blocks = own_ref.shape[0]
     groups = total_rows // ROWS
@@ -70,14 +71,12 @@
     fused = (level > 0) & (level != HANDED + 1)
 
     def load(which, i):
-        source, target = ((finv_hbm, finv), (coup_hbm, coup), (upd_hbm, upd))[which]
+        source, target = ((finv_hbm, finv), (coup_hbm, coup), (upd_hbm, upd), (rhs_hbm, rhs_ref), (inc_hbm, inc_ref))[which]
         return pltpu.make_async_copy(source.at[i], target.at[i], load_sem.at[which, i])
 
     for i in range(fronts):
-        load(0, i).start()
-    for i in range(fronts):
-        load(1, i).start()
-        load(2, i).start()
+        for which in (3, 4, 1, 0, 2):
+            load(which, i).start()
 
     barrier = pltpu.get_barrier_semaphore()
 
@@ -206,10 +205,10 @@
     def begin(b, carry):
         these = [b * TOGETHER + n for n in range(TOGETHER)]
         for i in these:
-            for which in range(3):
+            for which in range(5):
                 load(which, i).wait()
         entering = [expand(packed(inc_ref[i])) for i in these]
-        fields = [packed(rhs_ref[0, i]) for i in these]
+        fields = [packed(rhs_ref[i]) for i in these]
         fields = [
             field - starts * collapse(dot(x, flat(coup, i))) for i, x, field in zip(these, entering, fields)
         ]
@@ -265,34 +264,37 @@
         take[...] = jnp.where(fits, 1.0, 0.0).T.astype(BF16)[: fronts * UNIT]
 
     def step(g):
+        @pl.when((level == 0) & (g >= WINDOW))
+        def _():
+            wait_for(back.at[g - WINDOW], back_recv.at[g - WINDOW])
+
         @pl.when(level == 0)
         def _():
-            contrib[...] = rhs_u[g].astype(BF16)
+            sent[g] = dot(place[...], rhs_u[g].astype(BF16)).astype(BF16)
+
+        @pl.when(fused)
+        def _():
+            wait_for(above_field.at[g], field_recv.at[g])
+            wait_for(got.at[g], got_sem.at[g])
+
+        @pl.when(entry)
+        def _():
+            wait_for(entered.at[g], entered_recv.at[g])
 
         @pl.when(level > 0)
         def _():
-            @pl.when(fused)
-            def _():
-                wait_for(above_field.at[g], field_recv.at[g])
-                wait_for(got.at[g], got_sem.at[g])
-                rest[g] = (above_field[g] - dot(take[...], got[g])).astype(BF16)
-                hand_back(g).start()
-
-            @pl.when(entry)
-            def _():
-                wait_for(entered.at[g], entered_recv.at[g])
-                rest[g] = entered[g]
-
-            x = expand(rest[g].astype(F32))
+            summed = (above_field[g] - dot(take[...], got[g])).astype(BF16).astype(F32)
+            remainder = jnp.where(entry, entered[g].astype(F32), summed)
+            rest[g] = remainder.astype(BF16)
+            x = expand(remainder)
             values = []
             for i in range(fronts):
                 wide = dot(x[i * UNIT : (i + 1) * UNIT], comp_u[i])
                 for k in range(blocks):
                     at = (i * blocks + k) * UNIT
                     values.append(rhs_u[g, at : at + UNIT, :] - collapse(wide[:, k * width : (k + 1) * width]))
-            contrib[...] = jnp.concatenate(values, axis=0).astype(BF16)
-
-        sent[g] = dot(place[...], contrib[...]).astype(BF16)
+            contrib = jnp.concatenate(values, axis=0).astype(BF16)
+            sent[g] = dot(place[...], contrib).astype(BF16)
 
         @pl.when(jnp.logical_not(kept))
         def _():
@@ -302,6 +304,10 @@
         def _():
             spread(sent.at[g], last.at[g], sent_sem.at[g], last_sem.at[g], level, steps[:-1])
             last[g, mine, :] = sent[g, mine, :]
+
+        @pl.when(fused)
+        def _():
+            hand_back(g).start()
 
         @pl.when(level > 0)
         def _():
@@ -352,8 +358,11 @@
 
     @pl.when(jnp.logical_not(kept))
     def _():
-        for g in range(groups):
+        def returned(g, carry):
             wait_for(back.at[g], back_recv.at[g])
+            return carry
+
+        lax.fori_loop(jnp.where(level == 0, groups - WINDOW, 0), groups, returned, 0)
         for i in range(fronts):
             at = i * UNIT
             value = jnp.concatenate([back[g].astype(F32)[at : at + UNIT] for g in range(groups)], axis=0)
@@ -416,9 +425,11 @@
     return pl.pallas_call(
         functools.partial(kernel, leafs, sweeps),
         out_shape=jax.ShapeDtypeStruct(rhs.shape, BF16),
-        in_specs=[vmem, vmem, hbm, hbm, hbm, vmem, vmem],
+        in_specs=[hbm, hbm, hbm, hbm, hbm, vmem, vmem],
         out_specs=vmem,
         scratch_shapes=[
+            pltpu.VMEM(incoming.shape, BF16),
+            pltpu.VMEM(incoming.shape, BF16),
             pltpu.VMEM(front_inv.shape[1:], BF16),
             pltpu.VMEM(coupling.shape[1:], BF16),
             pltpu.VMEM(update.shape[1:], BF16),
@@ -429,7 +440,6 @@
             pltpu.VMEM((fronts * UNIT, slots), BF16),
             pltpu.VMEM((groups, fronts * UNIT, LANES), F32),
             pltpu.VMEM((groups, pairs * UNIT, LANES), F32),
-            pltpu.VMEM((pairs * UNIT, LANES), BF16),
             pltpu.VMEM((groups, fronts * UNIT, LANES), BF16),
             pltpu.VMEM((groups, fronts * UNIT, LANES), BF16),
             pltpu.VMEM((groups, fronts * UNIT, LANES), F32),
@@ -441,7 +451,7 @@
             pltpu.VMEM((groups, slots, LANES), BF16),
             pltpu.VMEM((slots, LANES), BF16),
             pltpu.VMEM((slots, LANES), BF16),
-            dma((3, fronts)),
+            dma((5, fronts)),
             dma((fronts,)),
             dma((fronts,)),
             dma((groups,)),
@@ -459,7 +469,7 @@
         compiler_params=pltpu.CompilerParams(
             collective_id=0, has_side_effects=True, vmem_limit_bytes=60 * 1024 * 1024
         ),
-    )(rhs, incoming, front_inv[0], coupling[0], update[0], dest_owner.T, dest_front.T)
+    )(rhs[0], incoming, front_inv[0], coupling[0], update[0], dest_owner.T, dest_front.T)
 
 
 def solution(mesh):

time: 122 us -> 122 us (level)
  no operation moved by 1% of the time
where the time goes in v4:
time: 122 us
  Pallas kernels  120 us (98%)
  local copies, waits for them, and re-layouts  1.67 us (1%)
    pallas_call x1, Pallas kernels, body(): pl.pallas_call(functools.partial(kernel, leafs, sweeps), out_shape=jax.Sh...  120 us

profile of v4, /device:TPU:25, one launch (start us, length us, event | category | flops | bytes accessed | tf_op | source)
XLA Modules:
  0.0 121.6 jit_solution(324649955210795938)
XLA Ops:
  0.0 119.9 %shard_map.73 = bf16[1,8,32,512]{3,2,1,0:T(8,128)(2,1)} custom-call(bf16[8,32,512]{2,1,0:T(8,128)(2,1)} %bitcast.9, bf16[8,32,512]{2,1,0:T(8,128)(2,1)} %inc_hbm.1, bf16[8,2,256,256]{3,2,1,0:T(8,128)(2,1)} %bitcast.7, bf16[8,2,256,256]{3,2,1,0:T(8,128)(2,1)} %bitcast.8, bf16[8,4,2,256,256]{4,3,2,1,0:T(8,128)(2,1)} %bitcast.6, s32[4,8]{1,0:T(4,128)} %bitcast.10, ...), custom_call_target="tpu_custom_call" | custom-call | tf_op jit(solution)/shard_map/pallas_call | solution.py:425
  119.9 1.7 %copy.9 = bf16[1,8,32,512]{3,2,1,0:T(8,128)(2,1)} copy(bf16[1,8,32,512]{3,2,1,0:T(8,128)(2,1)} %shard_map.73) | data formatting | bytes 524288

commit v5 on v4

--- a/solution.py
+++ b/solution.py
@@ -296,6 +296,10 @@
             contrib = jnp.concatenate(values, axis=0).astype(BF16)
             sent[g] = dot(place[...], contrib).astype(BF16)
 
+        @pl.when(fused)
+        def _():
+            hand_back(g).start()
+
         @pl.when(jnp.logical_not(kept))
         def _():
             spread(sent.at[g], got.at[g], sent_sem.at[g], got_sem.at[g], level + 1, steps)
@@ -304,10 +308,6 @@
         def _():
             spread(sent.at[g], last.at[g], sent_sem.at[g], last_sem.at[g], level, steps[:-1])
             last[g, mine, :] = sent[g, mine, :]
-
-        @pl.when(fused)
-        def _():
-            hand_back(g).start()
 
         @pl.when(level > 0)
         def _():

time: 122 us -> 121 us (level)
  no operation moved by 1% of the time
where the time goes in v5:
time: 121 us
  Pallas kernels  119 us (98%)
  local copies, waits for them, and re-layouts  1.67 us (1%)
    pallas_call x1, Pallas kernels, body(): pl.pallas_call(functools.partial(kernel, leafs, sweeps), out_shape=jax.Sh...  119 us

profile of v5, /device:TPU:25, one launch (start us, length us, event | category | flops | bytes accessed | tf_op | source)
XLA Modules:
  0.0 120.8 jit_solution(6021223881157247205)
XLA Ops:
  0.0 119.2 %shard_map.73 = bf16[1,8,32,512]{3,2,1,0:T(8,128)(2,1)} custom-call(bf16[8,32,512]{2,1,0:T(8,128)(2,1)} %bitcast.9, bf16[8,32,512]{2,1,0:T(8,128)(2,1)} %inc_hbm.1, bf16[8,2,256,256]{3,2,1,0:T(8,128)(2,1)} %bitcast.7, bf16[8,2,256,256]{3,2,1,0:T(8,128)(2,1)} %bitcast.8, bf16[8,4,2,256,256]{4,3,2,1,0:T(8,128)(2,1)} %bitcast.6, s32[4,8]{1,0:T(4,128)} %bitcast.10, ...), custom_call_target="tpu_custom_call" | custom-call | tf_op jit(solution)/shard_map/pallas_call | solution.py:425
  119.2 1.7 %copy.9 = bf16[1,8,32,512]{3,2,1,0:T(8,128)(2,1)} copy(bf16[1,8,32,512]{3,2,1,0:T(8,128)(2,1)} %shard_map.73) | data formatting | bytes 524288
